TPU v7x, 32 devices: a whole 2x2x4 slice. The times are simulated.
32 devices in a mesh: row: 8 (over z, core), col: 4 (over y, x).
Axes of the slice: x: 2, y: 2, z: 4, core: 2. Of those that a mesh axis runs over, the one named last changes fastest.
Arguments:
- features: bfloat16 [192, 96, 256], P('row', 'col'), may hold values from -6 to 6
- kernels: bfloat16 [4608, 128], P('row', 'col'), may hold values from -0.125 to 0.125
- out_cotangent: bfloat16 [2, 192, 96, 128], P(None, 'row', 'col'), may hold values from -6 to 6
Outputs:
- branch_maps: bfloat16 [2, 192, 96, 128], P(None, 'row', 'col')
- input_grad: bfloat16 [192, 96, 256], P('row', 'col')
- kernel_grad: float32 [4608, 128], P('row', 'col')
All inputs are finite; a program needn't handle non-finite values.
Results may differ from a plain program's by a relative error of at most 0.001.
Values may be sent and summed in bfloat16 or wider, within the bound.
A program may use at most 64 MiB of HBM per device.

v0:
```python
import jax
import jax.numpy as jnp
from jax import lax
from jax.sharding import PartitionSpec as P

FIRST_SPACING = 12
SECOND_SPACING = 24


def with_halo(x, sides, width):
    for axis, dim in sides:
        size, length = (lax.axis_size(axis), x.shape[dim])
        up = [(i, (i + 1) % size) for i in range(size - 1)]
        down = [(j, i) for i, j in up]
        last = lax.slice_in_dim(x, length - width, length, axis=dim)
        initial = lax.slice_in_dim(x, 0, width, axis=dim)
        before = lax.ppermute(last, axis, up)
        after = lax.ppermute(initial, axis, down)
        x = jnp.concatenate([before, x, after], axis=dim)
    return x


def local(features, kernels, out_cotangent):
    rows_dev = features.shape[0]
    cols_dev = features.shape[1]
    chans = features.shape[2]
    outs_n = out_cotangent.shape[3]
    padding_margin = SECOND_SPACING
    x_ext = with_halo(features, (("row", 0), ("col", 1)), padding_margin)
    g_ext = with_halo(out_cotangent, (("row", 1), ("col", 2)), padding_margin)
    w_cols = lax.all_gather(kernels, "col", axis=1, tiled=True)
    w_full = lax.all_gather(w_cols, "row", axis=0, tiled=True)
    w_blocks = w_full.reshape(2, 9, chans, outs_n)
    pixels = rows_dev * cols_dev
    maps = []
    grads = []
    grad_in = jnp.zeros((pixels, chans), jnp.float32)
    for branch_index, dilation_rate in ((0, FIRST_SPACING), (1, SECOND_SPACING)):
        result = jnp.zeros((pixels, outs_n), jnp.float32)
        g_flat = out_cotangent[branch_index].reshape(pixels, outs_n)
        for kernel_tap in range(9):
            shift_down = (kernel_tap // 3 - 1) * dilation_rate
            shift_across = (kernel_tap % 3 - 1) * dilation_rate
            x_tap = x_ext[
                padding_margin + shift_down : padding_margin + shift_down + rows_dev,
                padding_margin + shift_across : padding_margin + shift_across + cols_dev,
            ].reshape(pixels, chans)
            g_tap = g_ext[
                branch_index,
                padding_margin - shift_down : padding_margin - shift_down + rows_dev,
                padding_margin - shift_across : padding_margin - shift_across + cols_dev,
            ].reshape(pixels, outs_n)
            weight = w_blocks[branch_index, kernel_tap]
            result = result + jnp.dot(x_tap, weight, preferred_element_type=jnp.float32)
            grad_in = grad_in + lax.dot_general(
                g_tap, weight, (((1,), (1,)), ((), ())), preferred_element_type=jnp.float32
            )
            grads.append(
                lax.dot_general(
                    x_tap, g_flat, (((0,), (0,)), ((), ())), preferred_element_type=jnp.float32
                )
            )
        maps.append(result.reshape(rows_dev, cols_dev, outs_n).astype(jnp.bfloat16))
    branch_maps = jnp.stack(maps, 0)
    input_grad = grad_in.reshape(rows_dev, cols_dev, chans).astype(jnp.bfloat16)
    local_grad = jnp.concatenate(grads, 0)
    total_cells = rows_dev * lax.axis_size("row") * cols_dev * lax.axis_size("col")
    scale = 1.0 / jnp.sqrt(jnp.float32(total_cells))
    partial_grad = lax.psum_scatter(local_grad, "row", scatter_dimension=0, tiled=True)
    kernel_grad = lax.psum_scatter(partial_grad, "col", scatter_dimension=1, tiled=True)
    return (branch_maps, input_grad, kernel_grad * scale)


def solution(mesh):
    placed = (P("row", "col", None), P("row", "col"), P(None, "row", "col", None))
    return jax.shard_map(
        local,
        mesh=mesh,
        in_specs=placed,
        out_specs=(P(None, "row", "col", None), P("row", "col", None), P("row", "col")),
        check_vma=False,
    )
```

profile of v0, /device:TPU:0, one launch (start us, length us, event | category | flops | bytes accessed | tf_op | source)
XLA Modules:
  0.0 169.9 jit_solution(2725577153025200455)
XLA Ops:
  7.2 1.4 collective-permute-start.1
  8.7 3.0 %collective-permute-start = (bf16[24,24,256]{2,1,0:T(8,128)(2,1)}, bf16[24,24,256]{2,1,0:T(8,128)(2,1)S(1)}, u32[]{:S(2)}, u32[]{:S(2)}) collective-permute-start(bf16[24,24,256]{2,1,0:T(8,128)(2,1)} %param.3), channel_id=1, source_target_pairs={{0,4},{4,8},{8,12},{12,16},{16,20},{20,24},{24,28},{1,5},{5,9},{9,... | collective-permute-start | bytes 884744 | tf_op jit(solution)/shard_map/ppermute | solution.py:17
  11.7 4.5 %collective-permute-start.4 = (bf16[2,24,24,128]{3,2,1,0:T(8,128)(2,1)}, bf16[2,24,24,128]{3,2,1,0:T(8,128)(2,1)S(1)}, u32[]{:S(2)}, u32[]{:S(2)}) collective-permute-start(bf16[2,24,24,128]{3,2,1,0:T(8,128)(2,1)} %param.5), channel_id=1, source_target_pairs={{0,4},{4,8},{8,12},{12,16},{16,20},{20,24},{24,28},{1,5},{5,9},{9,... | collective-permute-start | bytes 884744 | tf_op jit(solution)/shard_map/ppermute | solution.py:17
  16.3 2.0 %pad_maximum_fusion.6 = (bf16[24,24,256]{2,1,0:T(8,128)(2,1)}, bf16[72,24,256]{2,1,0:T(8,128)(2,1)}, bf16[24,24,256]{2,1,0:T(8,128)(2,1)}) fusion(bf16[24,24,256]{2,1,0:T(8,128)(2,1)} %param.3, bf16[24,24,256]{2,1,0:T(8,128)(2,1)S(1)} %collective-permute-done, bf16[24,24,256]{2,1,0:T(8,128)(2,1)S(1)} %collective-permute-done.1), kind=kLoop, calls=%fused_computation.60 | loop fusion | flops 1179647 | bytes 1769472 | tf_op jit(solution)/shard_map/concatenate | solution.py:19
  19.8 1.3 collective-permute-start.3
  21.1 4.6 %collective-permute-start.2 = (bf16[72,24,256]{2,1,0:T(8,128)(2,1)}, bf16[72,24,256]{2,1,0:T(8,128)(2,1)S(1)}, u32[]{:S(2)}, u32[]{:S(2)}) collective-permute-start(bf16[72,24,256]{2,1,0:T(8,128)(2,1)} %constant_dynamic-update-slice_fusion), channel_id=1, source_target_pairs={{0,1},{1,2},{2,3},{4,5},{5,6},{6,7},{8,9},{9,10},{10,11},{12,13},{... | collective-permute-start | bytes 2654216 | tf_op jit(solution)/shard_map/ppermute | solution.py:17
  25.7 1.3 collective-permute-start.5
  27.0 37.4 %all_gather.6 = bf16[576,128]{0,1:T(8,128)(2,1)S(1)} all-gather(bf16[576,32]{0,1:T(8,128)(2,1)S(1)} %copy-done.47), channel_id=1, replica_groups=mesh['row'=8,'col'=4] {'col'}, dimensions={1}, use_global_device_ids=true | all-gather | bytes 184320 | tf_op jit(solution)/shard_map/all_gather | solution.py:31
  67.7 6.1 %collective-permute-start.7 = (bf16[2,72,24,128]{3,2,1,0:T(8,128)(2,1)}, bf16[2,72,24,128]{3,2,1,0:T(8,128)(2,1)}, u32[]{:S(2)}, u32[]{:S(2)}) collective-permute-start(bf16[2,72,24,128]{3,2,1,0:T(8,128)(2,1)} %constant_dynamic-update-slice_fusion.3), channel_id=1, source_target_pairs={{0,1},{1,2},{2,3},{4,5},{5,6},{6,7},{8,9},{9,10},{10,11},{12,13},{... | collective-permute-start | bytes 2654216 | tf_op jit(solution)/shard_map/ppermute | solution.py:17
  73.8 1.3 collective-permute-start.6
  75.9 2.4 %pad_maximum_fusion.3 = (bf16[24,24,256]{2,1,0:T(8,128)(2,1)S(1)}, bf16[24,24,256]{2,1,0:T(8,128)(2,1)S(1)}, bf16[24,24,256]{2,1,0:T(8,128)(2,1)S(1)}, bf16[24,2...) fusion(bf16[72,24,256]{2,1,0:T(8,128)(2,1)S(1)} %collective-per, ...), kind=kLoop, calls=%fused_computation.57 | loop fusion | flops 3538944 | bytes 7962624 | tf_op jit(solution)/shard_map/slice | solution.py:44
  78.4 1.3 convolution_dynamic-update-slice_fusion.17
  79.8 1.0 convolution_dynamic-update-slice_fusion.16
  81.7 0.9 convolution_dynamic-update-slice_fusion.14
  83.6 0.9 convolution_dynamic-update-slice_fusion.12
  85.5 1.0 convolution_dynamic-update-slice_fusion.10
  86.4 1.0 convolution_dynamic-update-slice_fusion.9
  89.3 1.0 convolution_dynamic-update-slice_fusion.6
  91.2 1.0 convolution_dynamic-update-slice_fusion.4
  93.1 1.0 convolution_dynamic-update-slice_fusion.2
  95.0 0.9 convolution_dynamic-update-slice_fusion
  96.0 17.6 %collective-permute-done.6 = bf16[2,72,24,128]{3,2,1,0:T(8,128)(2,1)} collective-permute-done((bf16[2,72,24,128]{3,2,1,0:T(8,128)(2,1)}, bf16[2,72,24,128]{3,2,1,0:T(8,128)(2,1)}, u32[]{:S(2)}, u32[]{:S(2)}) %collective-permute-start.6) | collective-permute-done | bytes 884768 | tf_op jit(solution)/shard_map/ppermute | solution.py:18
  113.6 2.9 %pad_maximum_fusion.12 = (bf16[1,24,24,128]{3,2,1,0:T(8,128)(2,1)}, bf16[1,24,24,128]{3,2,1,0:T(8,128)(2,1)}, bf16[1,24,24,128]{3,2,1,0:T(8,128)(2,1)}, bf16[1,2...) fusion(bf16[2,72,24,128]{3,2,1,0:T(8,128)(2,1)} %constant_dynam, ...), kind=kLoop, calls=%fused_computation.66 | loop fusion | flops 1769472 | bytes 5308416 | tf_op jit(solution)/shard_map/slice | solution.py:48
  116.5 1.2 fusion.51
  117.7 1.1 fusion.36
  123.4 1.1 fusion.54
  125.9 1.0 fusion.52
  131.9 3.4 %reduce-scatter.5.cloned.1.call-done = f32[576,128]{1,0:T(8,128)} async-done(((f32[4608,128]{1,0:T(8,128)}), f32[576,128]{1,0:T(8,128)}) %reduce-scatter.5.cloned.1.call-update) | async-done | bytes 294928 | tf_op jit(solution)/shard_map/reduce_scatter | solution.py:69
  135.3 1.9 %copy.11 = f32[576,128]{0,1:T(8,128)} copy(f32[576,128]{1,0:T(8,128)} %reduce-scatter.5.cloned.1.call-done) | data formatting | bytes 589824
  138.2 1.0 fusion.14
  139.2 22.3 %reduce-scatter.7.cloned.1.call-done = f32[32,576]{1,0:T(8,128)} async-done(((f32[128,576]{1,0:T(8,128)}), f32[32,576]{1,0:T(8,128)}) %reduce-scatter.7.cloned.1.call-update) | async-done | bytes 73744
  161.6 1.0 copy.12
  (159 shorter events, 25.6 us)
Async XLA Ops:
  7.2 11.2 %copy-start = (bf16[24,24,256]{2,1,0:T(8,128)(2,1)S(1)}, bf16[24,24,256]{2,1,0:T(8,128)(2,1)}, u32[]{:S(2)}) copy-start(bf16[24,24,256]{2,1,0:T(8,128)(2,1)} %param.3) | copy-start | bytes 884740
  7.2 18.6 %copy-start.27 = (bf16[2,24,24,128]{3,2,1,0:T(8,128)(2,1)S(1)}, bf16[2,24,24,128]{3,2,1,0:T(8,128)(2,1)}, u32[]{:S(2)}) copy-start(bf16[2,24,24,128]{3,2,1,0:T(8,128)(2,1)} %param.5) | copy-start | bytes 884740
  7.2 19.9 %copy-start.47 = (bf16[576,32]{0,1:T(8,128)(2,1)S(1)}, bf16[576,32]{0,1:T(8,128)(2,1)}, u32[]{:S(2)}) copy-start(bf16[576,32]{0,1:T(8,128)(2,1)} %param.4) | copy-start | bytes 110596
  7.2 109.3 %all-gather.2.cloned.1.call-start = ((), (), s32[]{:S(2)}) async-start(), calls=%async_computation.2 | async-start | bytes 1327104 | tf_op jit(solution)/shard_map/all_gather | solution.py:32
  7.2 9.0 %collective-permute-start.1 = (bf16[24,24,256]{2,1,0:T(8,128)(2,1)}, bf16[24,24,256]{2,1,0:T(8,128)(2,1)S(1)}, u32[]{:S(2)}, u32[]{:S(2)}) collective-permute-start(bf16[24,24,256]{2,1,0:T(8,128)(2,1)} %param.3), channel_id=1, source_target_pairs={{4,0},{8,4},{12,8},{16,12},{20,16},{24,20},{28,24},{5,1},{9,5},{13... | collective-permute-start | bytes 884744 | tf_op jit(solution)/shard_map/ppermute | solution.py:18
  8.7 7.6 %collective-permute-start = (bf16[24,24,256]{2,1,0:T(8,128)(2,1)}, bf16[24,24,256]{2,1,0:T(8,128)(2,1)S(1)}, u32[]{:S(2)}, u32[]{:S(2)}) collective-permute-start(bf16[24,24,256]{2,1,0:T(8,128)(2,1)} %param.3), channel_id=1, source_target_pairs={{0,4},{4,8},{8,12},{12,16},{16,20},{20,24},{24,28},{1,5},{5,9},{9,... | collective-permute-start | bytes 884744 | tf_op jit(solution)/shard_map/ppermute | solution.py:17
  11.7 53.6 %collective-permute-start.4 = (bf16[2,24,24,128]{3,2,1,0:T(8,128)(2,1)}, bf16[2,24,24,128]{3,2,1,0:T(8,128)(2,1)S(1)}, u32[]{:S(2)}, u32[]{:S(2)}) collective-permute-start(bf16[2,24,24,128]{3,2,1,0:T(8,128)(2,1)} %param.5), channel_id=1, source_target_pairs={{0,4},{4,8},{8,12},{12,16},{16,20},{20,24},{24,28},{1,5},{5,9},{9,... | collective-permute-start | bytes 884744 | tf_op jit(solution)/shard_map/ppermute | solution.py:17
  19.8 56.1 %collective-permute-start.3 = (bf16[72,24,256]{2,1,0:T(8,128)(2,1)}, bf16[72,24,256]{2,1,0:T(8,128)(2,1)S(1)}, u32[]{:S(2)}, u32[]{:S(2)}) collective-permute-start(bf16[72,24,256]{2,1,0:T(8,128)(2,1)} %constant_dynamic-update-slice_fusion), channel_id=1, source_target_pairs={{1,0},{2,1},{3,2},{5,4},{6,5},{7,6},{9,8},{10,9},{11,10},{13,12},{... | collective-permute-start | bytes 2654216 | tf_op jit(solution)/shard_map/ppermute | solution.py:18
  21.1 54.8 %collective-permute-start.2 = (bf16[72,24,256]{2,1,0:T(8,128)(2,1)}, bf16[72,24,256]{2,1,0:T(8,128)(2,1)S(1)}, u32[]{:S(2)}, u32[]{:S(2)}) collective-permute-start(bf16[72,24,256]{2,1,0:T(8,128)(2,1)} %constant_dynamic-update-slice_fusion), channel_id=1, source_target_pairs={{0,1},{1,2},{2,3},{4,5},{5,6},{6,7},{8,9},{9,10},{10,11},{12,13},{... | collective-permute-start | bytes 2654216 | tf_op jit(solution)/shard_map/ppermute | solution.py:17
  25.7 41.2 %collective-permute-start.5 = (bf16[2,24,24,128]{3,2,1,0:T(8,128)(2,1)S(1)}, bf16[2,24,24,128]{3,2,1,0:T(8,128)(2,1)S(1)}, u32[]{:S(2)}, u32[]{:S(2)}) collective-permute-start(bf16[2,24,24,128]{3,2,1,0:T(8,128)(2,1)S(1)} %copy-done.27), channel_id=1, source_target_pairs={{4,0},{8,4},{12,8},{16,12},{20,16},{24,20},{28,24},{5,1},{9,5},{13... | collective-permute-start | bytes 884744 | tf_op jit(solution)/shard_map/ppermute | solution.py:18
  65.3 70.0 %reduce-scatter.5.cloned.1.call-start = ((), (), s32[]{:S(2)}) async-start(), calls=%async_computation.3 | async-start | bytes 2654208 | tf_op jit(solution)/shard_map/reduce_scatter | solution.py:69
  67.7 28.3 %collective-permute-start.7 = (bf16[2,72,24,128]{3,2,1,0:T(8,128)(2,1)}, bf16[2,72,24,128]{3,2,1,0:T(8,128)(2,1)}, u32[]{:S(2)}, u32[]{:S(2)}) collective-permute-start(bf16[2,72,24,128]{3,2,1,0:T(8,128)(2,1)} %constant_dynamic-update-slice_fusion.3), channel_id=1, source_target_pairs={{0,1},{1,2},{2,3},{4,5},{5,6},{6,7},{8,9},{9,10},{10,11},{12,13},{... | collective-permute-start | bytes 2654216 | tf_op jit(solution)/shard_map/ppermute | solution.py:17
  73.8 39.8 %collective-permute-start.6 = (bf16[2,72,24,128]{3,2,1,0:T(8,128)(2,1)}, bf16[2,72,24,128]{3,2,1,0:T(8,128)(2,1)}, u32[]{:S(2)}, u32[]{:S(2)}) collective-permute-start(bf16[2,72,24,128]{3,2,1,0:T(8,128)(2,1)} %constant_dynamic-update-slice_fusion.3), channel_id=1, source_target_pairs={{1,0},{2,1},{3,2},{5,4},{6,5},{7,6},{9,8},{10,9},{11,10},{13,12},{... | collective-permute-start | bytes 2654216 | tf_op jit(solution)/shard_map/ppermute | solution.py:18
  75.9 3.8 %copy-start.25 = (bf16[24,24,256]{2,1,0:T(8,128)(2,1)S(1)}, bf16[24,24,256]{2,1,0:T(8,128)(2,1)}, u32[]{:S(2)}) copy-start(bf16[24,24,256]{2,1,0:T(8,128)(2,1)} %get-tuple-element.48) | copy-start | bytes 884740
  78.3 5.2 %copy-start.4 = (bf16[24,24,256]{2,1,0:T(8,128)(2,1)}, bf16[24,24,256]{2,1,0:T(8,128)(2,1)S(1)}, u32[]{:S(2)}) copy-start(bf16[24,24,256]{2,1,0:T(8,128)(2,1)S(1)} %get-tuple-element.35) | copy-start | bytes 884740
  78.3 5.2 %copy-start.14 = (bf16[24,24,256]{2,1,0:T(8,128)(2,1)}, bf16[24,24,256]{2,1,0:T(8,128)(2,1)S(1)}, u32[]{:S(2)}) copy-start(bf16[24,24,256]{2,1,0:T(8,128)(2,1)S(1)} %get-tuple-element.34) | copy-start | bytes 884740
  78.3 5.2 %copy-start.2 = (bf16[24,24,256]{2,1,0:T(8,128)(2,1)}, bf16[24,24,256]{2,1,0:T(8,128)(2,1)S(1)}, u32[]{:S(2)}) copy-start(bf16[24,24,256]{2,1,0:T(8,128)(2,1)S(1)} %get-tuple-element.18) | copy-start | bytes 884740
  78.4 6.2 %copy-start.16 = (bf16[24,24,256]{2,1,0:T(8,128)(2,1)}, bf16[24,24,256]{2,1,0:T(8,128)(2,1)S(1)}, u32[]{:S(2)}) copy-start(bf16[24,24,256]{2,1,0:T(8,128)(2,1)S(1)} %get-tuple-element.33) | copy-start | bytes 884740
  78.4 8.1 %copy-start.18 = (bf16[24,24,256]{2,1,0:T(8,128)(2,1)}, bf16[24,24,256]{2,1,0:T(8,128)(2,1)S(1)}, u32[]{:S(2)}) copy-start(bf16[24,24,256]{2,1,0:T(8,128)(2,1)S(1)} %get-tuple-element.20) | copy-start | bytes 884740
  78.4 10.9 %copy-start.6 = (bf16[24,24,256]{2,1,0:T(8,128)(2,1)}, bf16[24,24,256]{2,1,0:T(8,128)(2,1)S(1)}, u32[]{:S(2)}) copy-start(bf16[24,24,256]{2,1,0:T(8,128)(2,1)S(1)} %get-tuple-element.41) | copy-start | bytes 884740
  78.4 11.8 %copy-start.10 = (bf16[24,24,256]{2,1,0:T(8,128)(2,1)}, bf16[24,24,256]{2,1,0:T(8,128)(2,1)S(1)}, u32[]{:S(2)}) copy-start(bf16[24,24,256]{2,1,0:T(8,128)(2,1)S(1)} %get-tuple-element.37) | copy-start | bytes 884740
  78.4 12.8 %copy-start.20 = (bf16[24,24,256]{2,1,0:T(8,128)(2,1)}, bf16[24,24,256]{2,1,0:T(8,128)(2,1)S(1)}, u32[]{:S(2)}) copy-start(bf16[24,24,256]{2,1,0:T(8,128)(2,1)S(1)} %get-tuple-element.19) | copy-start | bytes 884740
  78.4 14.7 %copy-start.12 = (bf16[24,24,256]{2,1,0:T(8,128)(2,1)}, bf16[24,24,256]{2,1,0:T(8,128)(2,1)S(1)}, u32[]{:S(2)}) copy-start(bf16[24,24,256]{2,1,0:T(8,128)(2,1)S(1)} %get-tuple-element.36) | copy-start | bytes 884740
  78.4 16.5 %copy-start.8 = (bf16[24,24,256]{2,1,0:T(8,128)(2,1)}, bf16[24,24,256]{2,1,0:T(8,128)(2,1)S(1)}, u32[]{:S(2)}) copy-start(bf16[24,24,256]{2,1,0:T(8,128)(2,1)S(1)} %get-tuple-element.39) | copy-start | bytes 884740
  81.7 3.8 %copy-start.24 = (bf16[24,24,256]{2,1,0:T(8,128)(2,1)S(1)}, bf16[24,24,256]{2,1,0:T(8,128)(2,1)}, u32[]{:S(2)}) copy-start(bf16[24,24,256]{2,1,0:T(8,128)(2,1)} %get-tuple-element.50) | copy-start | bytes 884740
  84.5 3.8 %copy-start.23 = (bf16[24,24,256]{2,1,0:T(8,128)(2,1)S(1)}, bf16[24,24,256]{2,1,0:T(8,128)(2,1)}, u32[]{:S(2)}) copy-start(bf16[24,24,256]{2,1,0:T(8,128)(2,1)} %copy-done.22) | copy-start | bytes 884740
  95.9 65.6 %reduce-scatter.7.cloned.1.call-start = ((), (), s32[]{:S(2)}) async-start(), calls=%async_computation.4 | async-start | bytes 409600
  131.5 5.8 %copy-start.34 = (bf16[576,128]{1,0:T(8,128)(2,1)S(1)}, bf16[576,128]{1,0:T(8,128)(2,1)}, u32[]{:S(2)}) copy-start(bf16[576,128]{1,0:T(8,128)(2,1)} %fusion.27) | copy-start | bytes 442372
  131.9 6.1 %copy-start.38 = (bf16[1,24,24,128]{3,2,1,0:T(8,128)(2,1)S(1)}, bf16[1,24,24,128]{3,2,1,0:T(8,128)(2,1)}, u32[]{:S(2)}) copy-start(bf16[1,24,24,128]{3,2,1,0:T(8,128)(2,1)} %get-tuple-element.31) | copy-start | bytes 442372
  131.9 6.3 %copy-start.28 = (f32[576,256]{1,0:T(8,128)S(1)}, f32[576,256]{1,0:T(8,128)}, u32[]{:S(2)}) copy-start(f32[576,256]{1,0:T(8,128)} %fusion.54) | copy-start | bytes 1769476
  131.9 6.3 %copy-start.29 = (f32[576,256]{1,0:T(8,128)S(1)}, f32[576,256]{1,0:T(8,128)}, u32[]{:S(2)}) copy-start(f32[576,256]{1,0:T(8,128)} %fusion.52) | copy-start | bytes 1769476
  131.9 6.3 %copy-start.35 = (bf16[1,24,24,128]{3,2,1,0:T(8,128)(2,1)S(1)}, bf16[1,24,24,128]{3,2,1,0:T(8,128)(2,1)}, u32[]{:S(2)}) copy-start(bf16[1,24,24,128]{3,2,1,0:T(8,128)(2,1)} %get-tuple-element.24) | copy-start | bytes 442372
  (27 other events, 33.8 us)
Sparse Core Ops, SparseCore 0:
  65.4 26.3 all-gather.1
  96.1 39.2 reduce-scatter.4
  138.1 23.4 reduce-scatter.6
where the time goes:
time: 171 us; the launch traced here: 170 us
  waiting for transfers between devices  43.4 us (25%)
  blocking collectives  37.4 us (22%)
  matrix products  30.7 us (18%)
  starting transfers between devices  23.7 us (14%)
  between operations  14.5 us (8%)
  local copies, waits for them, and re-layouts  11.2 us (7%)
  other arithmetic  8.92 us (5%)
    all_gather x1, blocking collectives, local(): w_cols = lax.all_gather(kernels, 'col', axis=1, tiled=True)  37.4 us
    unnamed x4, waiting for transfers between devices  22.4 us
    ppermute x4, starting transfers between devices, with_halo(): before = lax.ppermute(last, axis, up)  18.3 us
    ppermute x4, waiting for transfers between devices, with_halo(): after = lax.ppermute(initial, axis, down)  17.6 us
    dot_general x18, matrix products, local(): lax.dot_general(x_tap, g_flat, (((0,), (0,)), ((), ())), preferred_elemen...  17.4 us
    unnamed x102, local copies, waits for them, and re-layouts  8.93 us
    dot_general x18, matrix products, local(): lax.dot_general(g_tap, weight, (((1,), (1,)), ((), ())), preferred_elemen...  6.7 us
    dot_general x18, matrix products, local(): result = result + jnp.dot(x_tap, weight, preferred_element_type=jnp.float32)  6.55 us
  transfers between devices with their start and end apart: 11, of which 3 were waited for; matrix products, arithmetic and copies ran while one was open for 26% of the time, Pallas kernels for 0%

commit v1 on v0

--- a/solution.py
+++ b/solution.py
@@ -28,7 +28,14 @@
     padding_margin = SECOND_SPACING
     x_ext = with_halo(features, (("row", 0), ("col", 1)), padding_margin)
     g_ext = with_halo(out_cotangent, (("row", 1), ("col", 2)), padding_margin)
-    w_cols = lax.all_gather(kernels, "col", axis=1, tiled=True)
+    ways, here, step = (lax.axis_size("col"), lax.axis_index("col"), kernels.shape[1])
+    line, have = (kernels, 1)
+    while have < ways:
+        line = jnp.concatenate(
+            [line, lax.ppermute(line, "col", [(d, (d - have) % ways) for d in range(ways)])], axis=1
+        )
+        have = 2 * have
+    w_cols = jnp.roll(line, here * step, axis=1)
     w_full = lax.all_gather(w_cols, "row", axis=0, tiled=True)
     w_blocks = w_full.reshape(2, 9, chans, outs_n)
     pixels = rows_dev * cols_dev

time: 171 us -> 161 us (0.942)
  blocking collectives: 37.4 us -> 0 us
  starting transfers between devices: 23.7 us -> 38.6 us
  matrix products: 30.7 us -> 39.1 us
  local copies, waits for them, and re-layouts: 11.2 us -> 13.9 us
    all_gather x1 -> x0, blocking collectives: 37.4 us -> none  [local(): w_cols = lax.all_gather(kernels, 'col', axis=1, tiled=True)]
    ppermute x4, starting transfers between devices: 18.3 us -> 28.5 us  [with_halo(): before = lax.ppermute(last, axis, up)]
    dot_general x18, matrix products: 6.7 us -> 15.8 us  [local(): lax.dot_general(g_tap, weight, (((1,), (1,)), ((), ())), preferred_elemen...]
    ppermute x0 -> x2, waiting for transfers between devices: none -> 4.46 us  [local(): lax.ppermute(line, 'col', [(d, (d - have) % ways) for d in range(ways)])]
    ppermute x4, waiting for transfers between devices: 17.6 us -> 22 us  [with_halo(): after = lax.ppermute(initial, axis, down)]
    ppermute x0 -> x2, starting transfers between devices: none -> 4.45 us  [local(): lax.ppermute(line, 'col', [(d, (d - have) % ways) for d in range(ways)])]
    unnamed x4, waiting for transfers between devices: 22.4 us -> 18.2 us
    reduce_scatter x1, waiting for transfers between devices: 3.43 us -> 0.01 us  [local(): lax.psum_scatter(local_grad, 'row', scatter_dimension=0, tiled=True)]
  transfers between devices with their start and end apart: 11 -> 13, of which waited for: 3 -> 3; matrix products, arithmetic and copies ran while one was open for 26% -> 36% of each run, Pallas kernels for 0% -> 0%
where the time goes in v1:
time: 161 us; the launch traced here: 160 us
  waiting for transfers between devices  44.7 us (28%)
  matrix products  39.1 us (24%)
  starting transfers between devices  38.6 us (24%)
  between operations  14.4 us (9%)
  local copies, waits for them, and re-layouts  13.9 us (9%)
  other arithmetic  9.54 us (6%)
    ppermute x4, starting transfers between devices, with_halo(): before = lax.ppermute(last, axis, up)  28.5 us
    ppermute x4, waiting for transfers between devices, with_halo(): after = lax.ppermute(initial, axis, down)  22 us
    unnamed x4, waiting for transfers between devices  18.2 us
    dot_general x18, matrix products, local(): lax.dot_general(x_tap, g_flat, (((0,), (0,)), ((), ())), preferred_elemen...  17.4 us
    dot_general x18, matrix products, local(): lax.dot_general(g_tap, weight, (((1,), (1,)), ((), ())), preferred_elemen...  15.8 us
    unnamed x95, local copies, waits for them, and re-layouts  8.75 us
    dot_general x18, matrix products, local(): result = result + jnp.dot(x_tap, weight, preferred_element_type=jnp.float32)  5.87 us
    ppermute x4, starting transfers between devices, with_halo(): after = lax.ppermute(initial, axis, down)  5.26 us
  transfers between devices with their start and end apart: 13, of which 3 were waited for; matrix products, arithmetic and copies ran while one was open for 36% of the time, Pallas kernels for 0%

profile of v1, /device:TPU:0, one launch (start us, length us, event | category | flops | bytes accessed | tf_op | source)
XLA Modules:
  0.0 160.3 jit_solution(14531792034997506399)
XLA Ops:
  7.2 1.4 collective-permute-start.1
  8.7 3.1 %collective-permute-start = (bf16[24,24,256]{2,1,0:T(8,128)(2,1)}, bf16[24,24,256]{2,1,0:T(8,128)(2,1)S(1)}, u32[]{:S(2)}, u32[]{:S(2)}) collective-permute-start(bf16[24,24,256]{2,1,0:T(8,128)(2,1)} %param.3), channel_id=1, source_target_pairs={{0,4},{4,8},{8,12},{12,16},{16,20},{20,24},{24,28},{1,5},{5,9},{9,... | collective-permute-start | bytes 884744 | tf_op jit(solution)/shard_map/ppermute | solution.py:17
  12.6 3.9 %collective-permute-start.3 = (bf16[576,32]{1,0:T(8,128)(2,1)S(1)}, bf16[576,32]{1,0:T(8,128)(2,1)S(1)}, u32[]{:S(2)}, u32[]{:S(2)}) collective-permute-start(bf16[576,32]{1,0:T(8,128)(2,1)S(1)} %copy.14), channel_id=1, source_target_pairs={{0,3},{1,0},{2,1},{3,2},{4,7},{5,4},{6,5},{7,6},{8,11},{9,8},{10,9... | collective-permute-start | bytes 110600 | tf_op jit(solution)/shard_map/ppermute | solution.py:35
  16.6 2.8 %collective-permute-start.6 = (bf16[2,24,24,128]{3,2,1,0:T(8,128)(2,1)}, bf16[2,24,24,128]{3,2,1,0:T(8,128)(2,1)S(1)}, u32[]{:S(2)}, u32[]{:S(2)}) collective-permute-start(bf16[2,24,24,128]{3,2,1,0:T(8,128)(2,1)} %param.5), channel_id=1, source_target_pairs={{0,4},{4,8},{8,12},{12,16},{16,20},{20,24},{24,28},{1,5},{5,9},{9,... | collective-permute-start | bytes 884744 | tf_op jit(solution)/shard_map/ppermute | solution.py:17
  19.4 2.0 %pad_maximum_fusion.6 = (bf16[24,24,256]{2,1,0:T(8,128)(2,1)}, bf16[72,24,256]{2,1,0:T(8,128)(2,1)}, bf16[24,24,256]{2,1,0:T(8,128)(2,1)}) fusion(bf16[24,24,256]{2,1,0:T(8,128)(2,1)} %param.3, bf16[24,24,256]{2,1,0:T(8,128)(2,1)S(1)} %collective-permute-done, bf16[24,24,256]{2,1,0:T(8,128)(2,1)S(1)} %collective-permute-done.1), kind=kLoop, calls=%fused_computation.68 | loop fusion | flops 1179647 | bytes 1769472 | tf_op jit(solution)/shard_map/concatenate | solution.py:19
  22.9 1.3 collective-permute-start.5
  24.2 4.6 %collective-permute-start.2 = (bf16[72,24,256]{2,1,0:T(8,128)(2,1)}, bf16[72,24,256]{2,1,0:T(8,128)(2,1)S(1)}, u32[]{:S(2)}, u32[]{:S(2)}) collective-permute-start(bf16[72,24,256]{2,1,0:T(8,128)(2,1)} %constant_dynamic-update-slice_fusion), channel_id=1, source_target_pairs={{0,1},{1,2},{2,3},{4,5},{5,6},{6,7},{8,9},{9,10},{10,11},{12,13},{... | collective-permute-start | bytes 2654216 | tf_op jit(solution)/shard_map/ppermute | solution.py:17
  30.1 1.3 collective-permute-start.7
  31.5 4.5 %collective-permute-done.4 = bf16[576,64]{1,0:T(8,128)(2,1)} collective-permute-done((bf16[576,64]{1,0:T(8,128)(2,1)}, bf16[576,64]{1,0:T(8,128)(2,1)}, u32[]{:S(2)}, u32[]{:S(2)}) %collective-permute-start.4) | collective-permute-done | bytes 73760 | tf_op jit(solution)/shard_map/ppermute | solution.py:35
  35.9 2.0 %concatenate.56 = bf16[576,256]{1,0:T(8,128)(2,1)} concatenate(bf16[576,32]{1,0:T(8,128)(2,1)S(1)} %copy.14, bf16[576,32]{1,0:T(8,128)(2,1)S(1)} %collective-permute-done.3, bf16[576,64]{1,0:T(8,128)(2,1)} %collective-permute-done.4, bf16[576,32]{1,0:T(8,128)(2,1)S(1)} %copy.14, bf16[576,32]{1,0:T(8,128)(2,1)S(1)} %collective-permute-done.3, bf16[576,64]{1,0:T(8,128)(2,1)} %collective-permute-done.4), dimensions={1} | concatenate | bytes 589824 | tf_op jit(solution)/shard_map/jit(_roll_dynamic)/concatenate | solution.py:38
  37.9 1.7 %constant_dynamic-slice_fusion = bf16[576,128]{1,0:T(8,128)(2,1)} fusion(bf16[576,256]{1,0:T(8,128)(2,1)} %concatenate.56, s32[]{:T(128)S(6)} %select_n.14), kind=kLoop, calls=%fused_computation.128 | loop fusion | bytes 294916 | tf_op jit(solution)/shard_map/jit(_roll_dynamic)/dynamic_slice | solution.py:38
  42.0 18.1 %collective-permute-start.9 = (bf16[2,72,24,128]{3,2,1,0:T(8,128)(2,1)}, bf16[2,72,24,128]{3,2,1,0:T(8,128)(2,1)}, u32[]{:S(2)}, u32[]{:S(2)}) collective-permute-start(bf16[2,72,24,128]{3,2,1,0:T(8,128)(2,1)} %constant_dynamic-update-slice_fusion.3), channel_id=1, source_target_pairs={{0,1},{1,2},{2,3},{4,5},{5,6},{6,7},{8,9},{9,10},{10,11},{12,13},{... | collective-permute-start | bytes 2654216 | tf_op jit(solution)/shard_map/ppermute | solution.py:17
  60.1 1.3 collective-permute-start.8
  62.2 2.3 %pad_maximum_fusion.3 = (bf16[24,24,256]{2,1,0:T(8,128)(2,1)S(1)}, bf16[24,24,256]{2,1,0:T(8,128)(2,1)S(1)}, bf16[24,24,256]{2,1,0:T(8,128)(2,1)S(1)}, bf16[24,2...) fusion(bf16[72,24,256]{2,1,0:T(8,128)(2,1)S(1)} %collective-per, ...), kind=kLoop, calls=%fused_computation.65 | loop fusion | flops 3538944 | bytes 7962624 | tf_op jit(solution)/shard_map/slice | solution.py:51
  64.6 1.3 convolution_dynamic-update-slice_fusion.17
  82.3 22.0 %collective-permute-done.8 = bf16[2,72,24,128]{3,2,1,0:T(8,128)(2,1)} collective-permute-done((bf16[2,72,24,128]{3,2,1,0:T(8,128)(2,1)}, bf16[2,72,24,128]{3,2,1,0:T(8,128)(2,1)}, u32[]{:S(2)}, u32[]{:S(2)}) %collective-permute-start.8) | collective-permute-done | bytes 884768 | tf_op jit(solution)/shard_map/ppermute | solution.py:18
  104.3 2.8 %pad_maximum_fusion.12 = (bf16[1,24,24,128]{3,2,1,0:T(8,128)(2,1)}, bf16[1,24,24,128]{3,2,1,0:T(8,128)(2,1)}, bf16[1,24,24,128]{3,2,1,0:T(8,128)(2,1)}, bf16[1,2...) fusion(bf16[2,72,24,128]{3,2,1,0:T(8,128)(2,1)} %constant_dynam, ...), kind=kLoop, calls=%fused_computation.74 | loop fusion | flops 1769472 | bytes 5308416 | tf_op jit(solution)/shard_map/slice | solution.py:55
  107.2 1.2 convolution_bitcast_fusion.5
  108.4 1.1 convolution_bitcast_fusion.7
  114.4 1.0 convolution_bitcast_fusion
  115.4 1.1 convolution_bitcast_fusion.2
  116.7 1.1 fusion.41
  117.8 1.1 fusion.52
  118.9 1.1 fusion.48
  119.9 1.1 fusion.44
  121.0 1.1 fusion.37
  122.3 1.0 fusion.50
  123.3 1.1 fusion.46
  125.9 1.1 fusion.2
  127.1 1.9 %copy.17 = f32[576,128]{0,1:T(8,128)} copy(f32[576,128]{1,0:T(8,128)} %reduce-scatter.5.cloned.1.call-done) | data formatting | bytes 589824
  130.1 3.6 %fusion.15 = bf16[576,256]{1,0:T(8,128)(2,1)} fusion(f32[576,256]{1,0:T(8,128)} %fusion.52, f32[576,256]{1,0:T(8,128)S(1)} %copy-done.28, f32[576,256]{1,0:T(8,128)} %fusion.50, f32[576,256]{1,0:T(8,128)} %fusion.48, f32[576,256]{1,0:T(8,128)S(1)} %convolution_bitcast_fusion.1, f32[576,256]{1,0:T(8,128)} %fusion.46, f32[576,256]{1,0:T(8,128)} %fusion.44, ...), kind=kOutput, calls=%fused_computation.21 | convolution fusion | flops 39813120 | bytes 8175616 | tf_op jit(solution)/shard_map/dot_general | solution.py:62
  133.7 18.2 %reduce-scatter.7.cloned.1.call-done = f32[32,576]{1,0:T(8,128)} async-done(((f32[128,576]{1,0:T(8,128)}), f32[32,576]{1,0:T(8,128)}) %reduce-scatter.7.cloned.1.call-update) | async-done | bytes 73744
  (157 shorter events, 32.9 us)
Async XLA Ops:
  7.2 14.3 %copy-start = (bf16[24,24,256]{2,1,0:T(8,128)(2,1)S(1)}, bf16[24,24,256]{2,1,0:T(8,128)(2,1)}, u32[]{:S(2)}) copy-start(bf16[24,24,256]{2,1,0:T(8,128)(2,1)} %param.3) | copy-start | bytes 884740
  7.2 100.0 %all-gather.2.cloned.1.call-start = ((), (), s32[]{:S(2)}) async-start(), calls=%async_computation.2 | async-start | bytes 1327104 | tf_op jit(solution)/shard_map/all_gather | solution.py:39
  7.2 12.2 %collective-permute-start.1 = (bf16[24,24,256]{2,1,0:T(8,128)(2,1)}, bf16[24,24,256]{2,1,0:T(8,128)(2,1)S(1)}, u32[]{:S(2)}, u32[]{:S(2)}) collective-permute-start(bf16[24,24,256]{2,1,0:T(8,128)(2,1)} %param.3), channel_id=1, source_target_pairs={{4,0},{8,4},{12,8},{16,12},{20,16},{24,20},{28,24},{5,1},{9,5},{13... | collective-permute-start | bytes 884744 | tf_op jit(solution)/shard_map/ppermute | solution.py:18
  8.7 10.8 %collective-permute-start = (bf16[24,24,256]{2,1,0:T(8,128)(2,1)}, bf16[24,24,256]{2,1,0:T(8,128)(2,1)S(1)}, u32[]{:S(2)}, u32[]{:S(2)}) collective-permute-start(bf16[24,24,256]{2,1,0:T(8,128)(2,1)} %param.3), channel_id=1, source_target_pairs={{0,4},{4,8},{8,12},{12,16},{16,20},{20,24},{24,28},{1,5},{5,9},{9,... | collective-permute-start | bytes 884744 | tf_op jit(solution)/shard_map/ppermute | solution.py:17
  12.6 16.2 %collective-permute-start.3 = (bf16[576,32]{1,0:T(8,128)(2,1)S(1)}, bf16[576,32]{1,0:T(8,128)(2,1)S(1)}, u32[]{:S(2)}, u32[]{:S(2)}) collective-permute-start(bf16[576,32]{1,0:T(8,128)(2,1)S(1)} %copy.14), channel_id=1, source_target_pairs={{0,3},{1,0},{2,1},{3,2},{4,7},{5,4},{6,5},{7,6},{8,11},{9,8},{10,9... | collective-permute-start | bytes 110600 | tf_op jit(solution)/shard_map/ppermute | solution.py:35
  16.6 23.1 %collective-permute-start.6 = (bf16[2,24,24,128]{3,2,1,0:T(8,128)(2,1)}, bf16[2,24,24,128]{3,2,1,0:T(8,128)(2,1)S(1)}, u32[]{:S(2)}, u32[]{:S(2)}) collective-permute-start(bf16[2,24,24,128]{3,2,1,0:T(8,128)(2,1)} %param.5), channel_id=1, source_target_pairs={{0,4},{4,8},{8,12},{12,16},{16,20},{20,24},{24,28},{1,5},{5,9},{9,... | collective-permute-start | bytes 884744 | tf_op jit(solution)/shard_map/ppermute | solution.py:17
  21.5 8.7 %copy-start.27 = (bf16[2,24,24,128]{3,2,1,0:T(8,128)(2,1)S(1)}, bf16[2,24,24,128]{3,2,1,0:T(8,128)(2,1)}, u32[]{:S(2)}) copy-start(bf16[2,24,24,128]{3,2,1,0:T(8,128)(2,1)} %param.5) | copy-start | bytes 884740
  22.9 39.3 %collective-permute-start.5 = (bf16[72,24,256]{2,1,0:T(8,128)(2,1)}, bf16[72,24,256]{2,1,0:T(8,128)(2,1)S(1)}, u32[]{:S(2)}, u32[]{:S(2)}) collective-permute-start(bf16[72,24,256]{2,1,0:T(8,128)(2,1)} %constant_dynamic-update-slice_fusion), channel_id=1, source_target_pairs={{1,0},{2,1},{3,2},{5,4},{6,5},{7,6},{9,8},{10,9},{11,10},{13,12},{... | collective-permute-start | bytes 2654216 | tf_op jit(solution)/shard_map/ppermute | solution.py:18
  24.2 38.0 %collective-permute-start.2 = (bf16[72,24,256]{2,1,0:T(8,128)(2,1)}, bf16[72,24,256]{2,1,0:T(8,128)(2,1)S(1)}, u32[]{:S(2)}, u32[]{:S(2)}) collective-permute-start(bf16[72,24,256]{2,1,0:T(8,128)(2,1)} %constant_dynamic-update-slice_fusion), channel_id=1, source_target_pairs={{0,1},{1,2},{2,3},{4,5},{5,6},{6,7},{8,9},{9,10},{10,11},{12,13},{... | collective-permute-start | bytes 2654216 | tf_op jit(solution)/shard_map/ppermute | solution.py:17
  29.6 6.3 %collective-permute-start.4 = (bf16[576,64]{1,0:T(8,128)(2,1)}, bf16[576,64]{1,0:T(8,128)(2,1)}, u32[]{:S(2)}, u32[]{:S(2)}) collective-permute-start(bf16[576,64]{1,0:T(8,128)(2,1)} %pad_maximum_fusion.17), channel_id=1, source_target_pairs={{0,2},{1,3},{2,0},{3,1},{4,6},{5,7},{6,4},{7,5},{8,10},{9,11},{10,... | collective-permute-start | bytes 221192 | tf_op jit(solution)/shard_map/ppermute | solution.py:35
  30.1 11.1 %collective-permute-start.7 = (bf16[2,24,24,128]{3,2,1,0:T(8,128)(2,1)S(1)}, bf16[2,24,24,128]{3,2,1,0:T(8,128)(2,1)S(1)}, u32[]{:S(2)}, u32[]{:S(2)}) collective-permute-start(bf16[2,24,24,128]{3,2,1,0:T(8,128)(2,1)S(1)} %copy-done.27), channel_id=1, source_target_pairs={{4,0},{8,4},{12,8},{16,12},{20,16},{24,20},{28,24},{5,1},{9,5},{13... | collective-permute-start | bytes 884744 | tf_op jit(solution)/shard_map/ppermute | solution.py:18
  39.6 87.5 %reduce-scatter.5.cloned.1.call-start = ((), (), s32[]{:S(2)}) async-start(), calls=%async_computation.3 | async-start | bytes 2654208 | tf_op jit(solution)/shard_map/reduce_scatter | solution.py:76
  42.0 40.3 %collective-permute-start.9 = (bf16[2,72,24,128]{3,2,1,0:T(8,128)(2,1)}, bf16[2,72,24,128]{3,2,1,0:T(8,128)(2,1)}, u32[]{:S(2)}, u32[]{:S(2)}) collective-permute-start(bf16[2,72,24,128]{3,2,1,0:T(8,128)(2,1)} %constant_dynamic-update-slice_fusion.3), channel_id=1, source_target_pairs={{0,1},{1,2},{2,3},{4,5},{5,6},{6,7},{8,9},{9,10},{10,11},{12,13},{... | collective-permute-start | bytes 2654216 | tf_op jit(solution)/shard_map/ppermute | solution.py:17
  60.1 44.3 %collective-permute-start.8 = (bf16[2,72,24,128]{3,2,1,0:T(8,128)(2,1)}, bf16[2,72,24,128]{3,2,1,0:T(8,128)(2,1)}, u32[]{:S(2)}, u32[]{:S(2)}) collective-permute-start(bf16[2,72,24,128]{3,2,1,0:T(8,128)(2,1)} %constant_dynamic-update-slice_fusion.3), channel_id=1, source_target_pairs={{1,0},{2,1},{3,2},{5,4},{6,5},{7,6},{9,8},{10,9},{11,10},{13,12},{... | collective-permute-start | bytes 2654216 | tf_op jit(solution)/shard_map/ppermute | solution.py:18
  62.2 3.7 %copy-start.25 = (bf16[24,24,256]{2,1,0:T(8,128)(2,1)S(1)}, bf16[24,24,256]{2,1,0:T(8,128)(2,1)}, u32[]{:S(2)}) copy-start(bf16[24,24,256]{2,1,0:T(8,128)(2,1)} %get-tuple-element.48) | copy-start | bytes 884740
  64.5 5.2 %copy-start.12 = (bf16[24,24,256]{2,1,0:T(8,128)(2,1)}, bf16[24,24,256]{2,1,0:T(8,128)(2,1)S(1)}, u32[]{:S(2)}) copy-start(bf16[24,24,256]{2,1,0:T(8,128)(2,1)S(1)} %get-tuple-element.34) | copy-start | bytes 884740
  64.5 5.2 %copy-start.18 = (bf16[24,24,256]{2,1,0:T(8,128)(2,1)}, bf16[24,24,256]{2,1,0:T(8,128)(2,1)S(1)}, u32[]{:S(2)}) copy-start(bf16[24,24,256]{2,1,0:T(8,128)(2,1)S(1)} %get-tuple-element.19) | copy-start | bytes 884740
  64.5 6.1 %copy-start.14 = (bf16[24,24,256]{2,1,0:T(8,128)(2,1)}, bf16[24,24,256]{2,1,0:T(8,128)(2,1)S(1)}, u32[]{:S(2)}) copy-start(bf16[24,24,256]{2,1,0:T(8,128)(2,1)S(1)} %get-tuple-element.33) | copy-start | bytes 884740
  64.5 8.0 %copy-start.16 = (bf16[24,24,256]{2,1,0:T(8,128)(2,1)}, bf16[24,24,256]{2,1,0:T(8,128)(2,1)S(1)}, u32[]{:S(2)}) copy-start(bf16[24,24,256]{2,1,0:T(8,128)(2,1)S(1)} %get-tuple-element.20) | copy-start | bytes 884740
  64.5 9.0 %copy-start.20 = (bf16[24,24,256]{2,1,0:T(8,128)(2,1)}, bf16[24,24,256]{2,1,0:T(8,128)(2,1)S(1)}, u32[]{:S(2)}) copy-start(bf16[24,24,256]{2,1,0:T(8,128)(2,1)S(1)} %get-tuple-element.38) | copy-start | bytes 884740
  64.6 10.9 %copy-start.2 = (bf16[24,24,256]{2,1,0:T(8,128)(2,1)}, bf16[24,24,256]{2,1,0:T(8,128)(2,1)S(1)}, u32[]{:S(2)}) copy-start(bf16[24,24,256]{2,1,0:T(8,128)(2,1)S(1)} %get-tuple-element.41) | copy-start | bytes 884740
  64.6 11.8 %copy-start.8 = (bf16[24,24,256]{2,1,0:T(8,128)(2,1)}, bf16[24,24,256]{2,1,0:T(8,128)(2,1)S(1)}, u32[]{:S(2)}) copy-start(bf16[24,24,256]{2,1,0:T(8,128)(2,1)S(1)} %get-tuple-element.37) | copy-start | bytes 884740
  64.6 13.7 %copy-start.4 = (bf16[24,24,256]{2,1,0:T(8,128)(2,1)}, bf16[24,24,256]{2,1,0:T(8,128)(2,1)S(1)}, u32[]{:S(2)}) copy-start(bf16[24,24,256]{2,1,0:T(8,128)(2,1)S(1)} %get-tuple-element.40) | copy-start | bytes 884740
  64.6 14.6 %copy-start.10 = (bf16[24,24,256]{2,1,0:T(8,128)(2,1)}, bf16[24,24,256]{2,1,0:T(8,128)(2,1)S(1)}, u32[]{:S(2)}) copy-start(bf16[24,24,256]{2,1,0:T(8,128)(2,1)S(1)} %get-tuple-element.36) | copy-start | bytes 884740
  64.6 16.5 %copy-start.6 = (bf16[24,24,256]{2,1,0:T(8,128)(2,1)}, bf16[24,24,256]{2,1,0:T(8,128)(2,1)S(1)}, u32[]{:S(2)}) copy-start(bf16[24,24,256]{2,1,0:T(8,128)(2,1)S(1)} %get-tuple-element.39) | copy-start | bytes 884740
  67.8 3.8 %copy-start.24 = (bf16[24,24,256]{2,1,0:T(8,128)(2,1)S(1)}, bf16[24,24,256]{2,1,0:T(8,128)(2,1)}, u32[]{:S(2)}) copy-start(bf16[24,24,256]{2,1,0:T(8,128)(2,1)} %get-tuple-element.50) | copy-start | bytes 884740
  70.7 3.8 %copy-start.23 = (bf16[24,24,256]{2,1,0:T(8,128)(2,1)S(1)}, bf16[24,24,256]{2,1,0:T(8,128)(2,1)}, u32[]{:S(2)}) copy-start(bf16[24,24,256]{2,1,0:T(8,128)(2,1)} %copy-done.22) | copy-start | bytes 884740
  82.1 69.8 %reduce-scatter.7.cloned.1.call-start = ((), (), s32[]{:S(2)}) async-start(), calls=%async_computation.4 | async-start | bytes 409600
  116.7 3.2 %copy-start.38 = (bf16[1,24,24,128]{3,2,1,0:T(8,128)(2,1)S(1)}, bf16[1,24,24,128]{3,2,1,0:T(8,128)(2,1)}, u32[]{:S(2)}) copy-start(bf16[1,24,24,128]{3,2,1,0:T(8,128)(2,1)} %get-tuple-element.26) | copy-start | bytes 442372
  117.8 3.2 %copy-start.37 = (bf16[1,24,24,128]{3,2,1,0:T(8,128)(2,1)S(1)}, bf16[1,24,24,128]{3,2,1,0:T(8,128)(2,1)}, u32[]{:S(2)}) copy-start(bf16[1,24,24,128]{3,2,1,0:T(8,128)(2,1)} %get-tuple-element.27) | copy-start | bytes 442372
  118.9 3.2 %copy-start.36 = (bf16[1,24,24,128]{3,2,1,0:T(8,128)(2,1)S(1)}, bf16[1,24,24,128]{3,2,1,0:T(8,128)(2,1)}, u32[]{:S(2)}) copy-start(bf16[1,24,24,128]{3,2,1,0:T(8,128)(2,1)} %get-tuple-element.28) | copy-start | bytes 442372
  127.1 3.0 %copy-start.43 = (bf16[1,24,24,128]{3,2,1,0:T(8,128)(2,1)S(1)}, bf16[1,24,24,128]{3,2,1,0:T(8,128)(2,1)}, u32[]{:S(2)}) copy-start(bf16[1,24,24,128]{3,2,1,0:T(8,128)(2,1)} %get-tuple-element.12) | copy-start | bytes 442372
  (25 other events, 39.3 us)
Sparse Core Ops, SparseCore 0:
  39.7 35.6 all-gather.1
  82.2 41.5 reduce-scatter.4
  129.2 22.6 reduce-scatter.6
